TPU v7x, 512 devices: a whole 4x8x8 slice. The times are simulated.
512 devices in a mesh: ctx: 128 (over y, z, core), head: 4 (over x).
Axes of the slice: x: 4, y: 8, z: 8, core: 2. Of those that a mesh axis runs over, the one named last changes fastest.
Arguments:
- queries: bfloat16 [2, 16384, 8192], P(None, ('ctx', 'head')), may hold values from -25 to 25
- keys: bfloat16 [2, 16384, 1024], P(None, ('ctx', 'head')), may hold values from -5.5 to 5.5
- values: bfloat16 [2, 16384, 1024], P(None, ('ctx', 'head')), may hold values from -6 to 6
- doc_lengths: int32 [47], replicated, may hold values from 1 to 1408, 32768 in all
Outputs:
- attended: bfloat16 [2, 16384, 8192], P(None, ('ctx', 'head'))
All inputs are finite; a program needn't handle non-finite values.
Results may differ from a plain program's by a relative error of at most 0.0045.
Values may be sent and summed in bfloat16 or wider, within the bound.
A program may use at most 64 MiB of HBM per device.

v0:
```python
import math
import jax
import jax.numpy as jnp
from jax import lax
from jax.sharding import PartitionSpec as P

HD = 128
REACH = 11
NEG_FILL = -1e30


def partner(block, axis, distance):
    count = lax.axis_size(axis)
    route = []
    for low in range(count):
        high = low | 1 << distance
        if high != low and high < count:
            route += [(low, high), (high, low)]
    return lax.ppermute(block, axis, route)


def shifted(block, axis, distance):
    devices = range(lax.axis_size(axis))
    route = [(i - distance, i) for i in devices if i - distance in devices]
    return lax.ppermute(block, axis, route)


def doc_of(positions, ends):
    return jnp.sum((positions[:, None] >= ends[None, :]).astype(jnp.int32), axis=1)


def attend(query, query_pos, keys, values, key_pos, ends, head_dim):
    rows = query.shape[0]
    kv_count = keys.shape[1] // head_dim
    group = query.shape[1] // head_dim // kv_count
    stride = min(group, 4)
    scale = 1.0 / math.sqrt(head_dim)
    allowed = (
        (doc_of(query_pos, ends)[:, None] == doc_of(key_pos, ends)[None, :])
        & (key_pos[None, :] <= query_pos[:, None])
        & (key_pos[None, :] >= 0)
    )
    pieces = []
    for kv_head in range(kv_count):
        key_head = keys[:, kv_head * head_dim : (kv_head + 1) * head_dim]
        value_head = values[:, kv_head * head_dim : (kv_head + 1) * head_dim]
        for portion in range(group // stride):
            first = (kv_head * group + portion * stride) * head_dim
            query_part = query[:, first : first + stride * head_dim].reshape(rows, stride, head_dim)
            scores = (
                jnp.einsum("rhd,sd->hrs", query_part, key_head, preferred_element_type=jnp.float32)
                * scale
            )
            masked = jnp.where(allowed[None], scores, NEG_FILL)
            top = jnp.max(masked, axis=2, keepdims=True)
            weights = jnp.where(allowed[None], jnp.exp(masked - top), 0.0)
            total = jnp.sum(weights, axis=2)
            mixed = jnp.einsum(
                "hrs,sd->rhd",
                weights.astype(jnp.bfloat16),
                value_head,
                preferred_element_type=jnp.float32,
            )
            pieces.append((mixed / total.T[:, :, None]).reshape(rows, stride * head_dim))
    return jnp.concatenate(pieces, axis=1).astype(jnp.bfloat16)


def half_attention(query, query_start, blocks, ends, head_dim):
    rows = query.shape[0]
    count = blocks.shape[0]
    width = blocks.shape[2] // 2
    query_pos = query_start + jnp.arange(rows, dtype=jnp.int32)
    window = blocks.reshape(count * rows, 2 * width)
    key_pos = query_start - (count - 1) * rows + jnp.arange(count * rows, dtype=jnp.int32)
    return attend(query, query_pos, window[:, :width], window[:, width:], key_pos, ends, head_dim)


def per_device(queries, keys, values, doc_lengths):
    head_dim = HD
    ctx_count = lax.axis_size("ctx")
    ctx_pos = lax.axis_index("ctx")
    reach = min(REACH, ctx_count // 2)
    query_local, key_local, value_local = (
        lax.all_to_all(queries, "head", split_axis=2, concat_axis=1, tiled=True),
        lax.all_to_all(keys, "head", split_axis=2, concat_axis=1, tiled=True),
        lax.all_to_all(values, "head", split_axis=2, concat_axis=1, tiled=True),
    )
    keyval = jnp.concatenate([key_local, value_local], axis=2)
    ends = jnp.cumsum(doc_lengths)
    rows = query_local.shape[1]
    query_width = query_local.shape[2]
    moving = jnp.concatenate([query_local[1], keyval[1]], axis=1)
    for digit in range(ctx_count.bit_length() - 1):
        moving = partner(moving, "ctx", digit)
    query_upper = moving[:, :query_width]
    keyval_upper = moving[:, query_width:]
    keyval_lower = keyval[0]
    held_pair = jnp.stack([keyval_lower, keyval_upper])
    earlier = []
    later = []
    for distance in range(1, reach + 1):
        earlier.append(shifted(keyval_lower, "ctx", distance))
        later.append(shifted(held_pair, "ctx", -distance))
    lower_blocks = jnp.stack(
        [earlier[distance - 1] for distance in range(reach, 0, -1)] + [keyval_lower]
    )
    lower_source = jnp.stack(
        [earlier[-offset - 1] for offset in range(-reach, 0)]
        + [keyval_lower]
        + [later[offset - 1][0] for offset in range(1, reach + 1)]
    )
    upper_source = jnp.stack(
        [keyval_upper] + [later[offset - 1][1] for offset in range(1, reach + 1)]
    )
    back_steps = jnp.arange(reach, -1, -1, dtype=jnp.int32)
    upper_index = 2 * ctx_count - 1 - ctx_pos
    target = upper_index - back_steps
    from_upper = target >= ctx_count
    offsets = jnp.clip(target - ctx_pos + reach, 0, 2 * reach)
    upper_blocks = jnp.where(
        from_upper[:, None, None],
        jnp.take(upper_source, back_steps, axis=0),
        jnp.take(lower_source, offsets, axis=0),
    )
    lower_out = half_attention(query_local[0], ctx_pos * rows, lower_blocks, ends, head_dim)
    upper_out = half_attention(query_upper, upper_index * rows, upper_blocks, ends, head_dim)
    for digit in range(ctx_count.bit_length() - 1):
        upper_out = partner(upper_out, "ctx", digit)
    result = jnp.stack([lower_out, upper_out])
    return lax.all_to_all(result, "head", split_axis=1, concat_axis=2, tiled=True)


def solution(mesh):
    placed = (
        P(None, ("ctx", "head"), None),
        P(None, ("ctx", "head"), None),
        P(None, ("ctx", "head"), None),
        P(),
    )
    return jax.shard_map(
        per_device,
        mesh=mesh,
        in_specs=placed,
        out_specs=P(None, ("ctx", "head"), None),
        check_vma=False,
    )
```

profile of v0, /device:TPU:248, one launch (start us, length us, event | category | flops | bytes accessed | tf_op | source)
XLA Modules:
  0.0 679.8 jit_solution(1722678336049449839)
XLA Ops:
  2.5 4.3 all-to-all-start
  9.1 3.6 all-to-all-done
  12.7 3.3 all-to-all-start.1
  16.1 6.8 %copy.273 = bf16[2,32,8192]{1,0,2:T(2,128)(2,1)} copy(bf16[2,32,8192]{2,1,0:T(8,128)(2,1)S(1)} %copy-done.2) | data formatting | bytes 2097152 | tf_op args[0]
  22.9 6.4 reshape.438
  29.3 4.7 all-to-all-start.2
  35.8 11.6 %all-to-all-done.2 = bf16[4,2,65536]{2,1,0:T(2,128)(2,1)S(1)} async-done(((bf16[4,2,65536]{2,1,0:T(2,128)(2,1)}), bf16[4,2,65536]{2,1,0:T(2,128)(2,1)S(1)}, u32[]{:S(2)}, u32[]{:S(2)}) %all-to-all-start.2) | async-done | bytes 1048608 | tf_op jit(solution)/shard_map/all_to_all | solution.py:84
  47.4 3.5 reshape.439
  50.9 9.8 %copy.347 = bf16[2,32,4,2048]{3,2,1,0:T(4,128)(2,1)S(1)} copy(bf16[2,32,4,2048]{1,0,3,2:T(2,128)(2,1)} %bitcast.374) | data formatting | bytes 2097152 | tf_op jit(solution)/shard_map/all_to_all | solution.py:84
  62.5 1.9 collective-permute-start.11
  64.6 1.9 collective-permute-done.11
  66.5 1.9 collective-permute-start.12
  68.7 16.4 %collective-permute-done.12 = bf16[128,2560]{1,0:T(8,128)(2,1)S(1)} collective-permute-done((bf16[128,2560]{1,0:T(8,128)(2,1)S(1)}, bf16[128,2560]{1,0:T(8,128)(2,1)S(1)}, u32[]{:S(2)}, u32[]{:S(2)}) %collective-permute-start.12) | collective-permute-done | bytes 655392 | tf_op jit(solution)/shard_map/ppermute | solution.py:19
  85.1 1.9 collective-permute-start.13
  87.1 3.1 and_and_fusion
  91.5 26.4 %collective-permute-done.13 = bf16[128,2560]{1,0:T(8,128)(2,1)S(1)} collective-permute-done((bf16[128,2560]{1,0:T(8,128)(2,1)S(1)}, bf16[128,2560]{1,0:T(8,128)(2,1)S(1)}, u32[]{:S(2)}, u32[]{:S(2)}) %collective-permute-start.13) | collective-permute-done | bytes 655392 | tf_op jit(solution)/shard_map/ppermute | solution.py:19
  117.9 8.2 %collective-permute-start.14 = (bf16[128,2560]{1,0:T(8,128)(2,1)S(1)}, bf16[128,2560]{1,0:T(8,128)(2,1)S(1)}, u32[]{:S(2)}, u32[]{:S(2)}) collective-permute-start(bf16[128,2560]{1,0:T(8,128)(2,1)S(1)} %collective-permute-done.13), channel_id=1, source_target_pairs={{0,32},{32,0},{4,36},{36,4},{8,40},{40,8},{12,44},{44,12},{16,48},... | collective-permute-start | bytes 1966088 | tf_op jit(solution)/shard_map/ppermute | solution.py:19
  128.0 1.9 collective-permute-start.2
  129.9 1.9 collective-permute-start.3
  131.9 3.0 collective-permute-start.4
  134.9 29.1 %collective-permute-done.1 = bf16[128,512]{1,0:T(8,128)(2,1)S(1)} collective-permute-done((bf16[128,512]{1,0:T(8,128)(2,1)S(1)}, bf16[128,512]{1,0:T(8,128)(2,1)S(1)}, u32[]{:S(2)}, u32[]{:S(2)}) %collective-permute-start.1) | collective-permute-done | bytes 131104 | tf_op jit(solution)/shard_map/ppermute | solution.py:25
  164.1 14.2 %collective-permute-start.5 = (bf16[128,512]{1,0:T(8,128)(2,1)S(1)}, bf16[128,512]{1,0:T(8,128)(2,1)S(1)}, u32[]{:S(2)}, u32[]{:S(2)}) collective-permute-start(bf16[128,512]{1,0:T(8,128)(2,1)S(1)} %bitcast.389), channel_id=1, source_target_pairs={{0,24},{4,28},{8,32},{12,36},{16,40},{20,44},{24,48},{28,52},{32,5... | collective-permute-start | bytes 393224 | tf_op jit(solution)/shard_map/ppermute | solution.py:25
  178.3 5.7 collective-permute-start.6
  184.1 1.9 collective-permute-start.15
  186.0 10.9 %collective-permute-start.7 = (bf16[128,512]{1,0:T(8,128)(2,1)S(1)}, bf16[128,512]{1,0:T(8,128)(2,1)S(1)}, u32[]{:S(2)}, u32[]{:S(2)}) collective-permute-start(bf16[128,512]{1,0:T(8,128)(2,1)S(1)} %bitcast.391), channel_id=1, source_target_pairs={{0,16},{4,20},{8,24},{12,28},{16,32},{20,36},{24,40},{28,44},{32,4... | collective-permute-start | bytes 393224 | tf_op jit(solution)/shard_map/ppermute | solution.py:25
  197.0 23.4 %collective-permute-start.8 = (bf16[128,512]{1,0:T(8,128)(2,1)S(1)}, bf16[128,512]{1,0:T(8,128)(2,1)S(1)}, u32[]{:S(2)}, u32[]{:S(2)}) collective-permute-start(bf16[128,512]{1,0:T(8,128)(2,1)S(1)} %bitcast.392), channel_id=1, source_target_pairs={{0,12},{4,16},{8,20},{12,24},{16,28},{20,32},{24,36},{28,40},{32,4... | collective-permute-start | bytes 393224 | tf_op jit(solution)/shard_map/ppermute | solution.py:25
  220.4 5.7 collective-permute-start.9
  226.1 5.3 collective-permute-start.16
  231.4 1.9 collective-permute-start.10
  233.4 26.2 %collective-permute-done.16 = bf16[128,2560]{1,0:T(8,128)(2,1)S(1)} collective-permute-done((bf16[128,2560]{1,0:T(8,128)(2,1)S(1)}, bf16[128,2560]{1,0:T(8,128)(2,1)S(1)}, u32[]{:S(2)}, u32[]{:S(2)}) %collective-permute-start.16) | collective-permute-done | bytes 655392 | tf_op jit(solution)/shard_map/ppermute | solution.py:19
  259.6 5.7 collective-permute-start.17
  265.4 29.8 %collective-permute-done.17 = bf16[128,2560]{1,0:T(8,128)(2,1)S(1)} collective-permute-done((bf16[128,2560]{1,0:T(8,128)(2,1)S(1)}, bf16[128,2560]{1,0:T(8,128)(2,1)S(1)}, u32[]{:S(2)}, u32[]{:S(2)}) %collective-permute-start.17) | collective-permute-done | bytes 655392 | tf_op jit(solution)/shard_map/ppermute | solution.py:19
  295.4 3.0 collective-permute-start.18
  298.4 4.4 collective-permute-start.19
  302.9 1.9 collective-permute-start.20
  304.8 1.9 collective-permute-start.21
  306.7 1.9 collective-permute-start.22
  311.1 2.1 collective-permute-start.23
  313.2 1.6 slice_dynamic-update-slice_fusion.21
  314.9 2.5 collective-permute-start.24
  318.0 14.0 %collective-permute-start.25 = (bf16[2,128,512]{2,1,0:T(8,128)(2,1)S(1)}, bf16[2,128,512]{2,1,0:T(8,128)(2,1)S(1)}, u32[]{:S(2)}, u32[]{:S(2)}) collective-permute-start(bf16[2,128,512]{2,1,0:T(8,128)(2,1)S(1)} %pad_maximum_fusion.3), channel_id=1, source_target_pairs={{32,0},{36,4},{40,8},{44,12},{48,16},{52,20},{56,24},{60,28},{64,3... | collective-permute-start | bytes 786440 | tf_op jit(solution)/shard_map/ppermute | solution.py:25
  332.7 71.5 %collective-permute-start.26 = (bf16[2,128,512]{2,1,0:T(8,128)(2,1)S(1)}, bf16[2,128,512]{2,1,0:T(8,128)(2,1)S(1)}, u32[]{:S(2)}, u32[]{:S(2)}) collective-permute-start(bf16[2,128,512]{2,1,0:T(8,128)(2,1)S(1)} %pad_maximum_fusion.3), channel_id=1, source_target_pairs={{36,0},{40,4},{44,8},{48,12},{52,16},{56,20},{60,24},{64,28},{68,3... | collective-permute-start | bytes 786440 | tf_op jit(solution)/shard_map/ppermute | solution.py:25
  404.8 3.3 collective-permute-start.27
  408.8 4.8 collective-permute-start.28
  416.2 3.3 collective-permute-done.27
  420.2 15.3 %collective-permute-done.28 = bf16[2,128,512]{2,1,0:T(8,128)(2,1)S(1)} collective-permute-done((bf16[2,128,512]{2,1,0:T(8,128)(2,1)S(1)}, bf16[2,128,512]{2,1,0:T(8,128)(2,1)S(1)}, u32[]{:S(2)}, u32[]{:S(2)}) %collective-permute-start.28) | collective-permute-done | bytes 262176 | tf_op jit(solution)/shard_map/ppermute | solution.py:25
  437.0 2.5 gather_fusion.1
  439.5 2.6 fusion.48
  442.1 2.6 fusion.222
  455.3 5.6 collective-permute-start.29
  462.4 9.1 %collective-permute-start.30 = (bf16[128,2048]{1,0:T(8,128)(2,1)S(1)}, bf16[128,2048]{1,0:T(8,128)(2,1)S(1)}, u32[]{:S(2)}, u32[]{:S(2)}) collective-permute-start(bf16[128,2048]{1,0:T(8,128)(2,1)S(1)} %collective-permute-done.29), channel_id=1, source_target_pairs={{0,8},{8,0},{4,12},{12,4},{16,24},{24,16},{20,28},{28,20},{32,40},... | collective-permute-start | bytes 1572872 | tf_op jit(solution)/shard_map/ppermute | solution.py:19
  471.5 12.2 %collective-permute-done.30 = bf16[128,2048]{1,0:T(8,128)(2,1)S(1)} collective-permute-done((bf16[128,2048]{1,0:T(8,128)(2,1)S(1)}, bf16[128,2048]{1,0:T(8,128)(2,1)S(1)}, u32[]{:S(2)}, u32[]{:S(2)}) %collective-permute-start.30) | collective-permute-done | bytes 524320 | tf_op jit(solution)/shard_map/ppermute | solution.py:19
  483.7 1.9 collective-permute-start.31
  486.1 25.2 %collective-permute-done.31 = bf16[128,2048]{1,0:T(8,128)(2,1)} collective-permute-done((bf16[128,2048]{1,0:T(8,128)(2,1)S(1)}, bf16[128,2048]{1,0:T(8,128)(2,1)}, u32[]{:S(2)}, u32[]{:S(2)}) %collective-permute-start.31) | collective-permute-done | bytes 524320 | tf_op jit(solution)/shard_map/ppermute | solution.py:19
  511.3 1.9 collective-permute-start.32
  513.2 2.5 fusion.226
  517.5 21.3 %collective-permute-done.32 = bf16[128,2048]{1,0:T(8,128)(2,1)} collective-permute-done((bf16[128,2048]{1,0:T(8,128)(2,1)}, bf16[128,2048]{1,0:T(8,128)(2,1)}, u32[]{:S(2)}, u32[]{:S(2)}) %collective-permute-start.32) | collective-permute-done | bytes 524320 | tf_op jit(solution)/shard_map/ppermute | solution.py:19
  538.8 19.3 %collective-permute-start.33 = (bf16[128,2048]{1,0:T(8,128)(2,1)}, bf16[128,2048]{1,0:T(8,128)(2,1)}, u32[]{:S(2)}, u32[]{:S(2)}) collective-permute-start(bf16[128,2048]{1,0:T(8,128)(2,1)} %collective-permute-done.32), channel_id=1, source_target_pairs={{0,64},{64,0},{4,68},{68,4},{8,72},{72,8},{12,76},{76,12},{16,80},... | collective-permute-start | bytes 1572872 | tf_op jit(solution)/shard_map/ppermute | solution.py:19
  561.3 9.3 %collective-permute-done.33 = bf16[128,2048]{1,0:T(8,128)(2,1)} collective-permute-done((bf16[128,2048]{1,0:T(8,128)(2,1)}, bf16[128,2048]{1,0:T(8,128)(2,1)}, u32[]{:S(2)}, u32[]{:S(2)}) %collective-permute-start.33) | collective-permute-done | bytes 524320 | tf_op jit(solution)/shard_map/ppermute | solution.py:19
  570.5 9.3 %collective-permute-start.34 = (bf16[128,2048]{1,0:T(8,128)(2,1)}, bf16[128,2048]{1,0:T(8,128)(2,1)}, u32[]{:S(2)}, u32[]{:S(2)}) collective-permute-start(bf16[128,2048]{1,0:T(8,128)(2,1)} %collective-permute-done.33), channel_id=1, source_target_pairs={{0,128},{128,0},{4,132},{132,4},{8,136},{136,8},{12,140},{140,12},... | collective-permute-start | bytes 1572872 | tf_op jit(solution)/shard_map/ppermute | solution.py:19
  582.9 19.0 %collective-permute-done.34 = bf16[128,2048]{1,0:T(8,128)(2,1)} collective-permute-done((bf16[128,2048]{1,0:T(8,128)(2,1)}, bf16[128,2048]{1,0:T(8,128)(2,1)}, u32[]{:S(2)}, u32[]{:S(2)}) %collective-permute-start.34) | collective-permute-done | bytes 524320 | tf_op jit(solution)/shard_map/ppermute | solution.py:19
  601.9 34.6 %collective-permute-start.35 = (bf16[128,2048]{1,0:T(8,128)(2,1)}, bf16[128,2048]{1,0:T(8,128)(2,1)S(1)}, u32[]{:S(2)}, u32[]{:S(2)}) collective-permute-start(bf16[128,2048]{1,0:T(8,128)(2,1)} %collective-permute-done.34), channel_id=1, source_target_pairs={{0,256},{256,0},{4,260},{260,4},{8,264},{264,8},{12,268},{268,12},... | collective-permute-start | bytes 1572872 | tf_op jit(solution)/shard_map/ppermute | solution.py:19
  639.6 20.4 %collective-permute-done.35 = bf16[128,2048]{1,0:T(8,128)(2,1)S(1)} collective-permute-done((bf16[128,2048]{1,0:T(8,128)(2,1)}, bf16[128,2048]{1,0:T(8,128)(2,1)S(1)}, u32[]{:S(2)}, u32[]{:S(2)}) %collective-permute-start.35) | collective-permute-done | bytes 524320 | tf_op jit(solution)/shard_map/ppermute | solution.py:19
  661.1 17.3 %all_to_all.69 = bf16[2,128,2048]{2,0,1:T(2,128)(2,1)S(1)} all-to-all(bf16[2,128,2048]{2,0,1:T(2,128)(2,1)S(1)} %copy.317), channel_id=1, replica_groups=mesh['ctx'=128,'head'=4] {'head'}, dimensions={1} | all-to-all | bytes 2097152 | tf_op jit(solution)/shard_map/all_to_all | solution.py:130
  (145 shorter events, 48.1 us)
Async XLA Ops:
  0.0 16.1 %copy-start.2 = (bf16[2,32,8192]{2,1,0:T(8,128)(2,1)S(1)}, bf16[2,32,8192]{2,1,0:T(8,128)(2,1)}, u32[]{:S(2)}) copy-start(bf16[2,32,8192]{2,1,0:T(8,128)(2,1)} %param.4) | copy-start | bytes 3145732
  2.5 10.3 %all-to-all-start = ((bf16[4,2,8192]{2,1,0:T(2,128)(2,1)}), bf16[4,2,8192]{2,1,0:T(2,128)(2,1)S(1)}, u32[]{:S(2)}, u32[]{:S(2)}) async-start(bf16[4,2,8192]{2,1,0:T(2,128)(2,1)} %reshape.434), calls=%async_computation | async-start | bytes 262144 | tf_op jit(solution)/shard_map/all_to_all | solution.py:85
  12.7 16.6 %all-to-all-start.1 = ((bf16[4,2,8192]{2,1,0:T(2,128)(2,1)}), bf16[4,2,8192]{2,1,0:T(2,128)(2,1)S(1)}, u32[]{:S(2)}, u32[]{:S(2)}) async-start(bf16[4,2,8192]{2,1,0:T(2,128)(2,1)} %reshape.436), calls=%async_computation.1 | async-start | bytes 262144 | tf_op jit(solution)/shard_map/all_to_all | solution.py:86
  22.9 11.1 %copy-start.11 = (s32[47]{0:T(128)S(1)}, s32[47]{0:T(128)}, u32[]{:S(2)}) copy-start(s32[47]{0:T(128)} %param.7) | copy-start | bytes 568
  29.3 18.1 %all-to-all-start.2 = ((bf16[4,2,65536]{2,1,0:T(2,128)(2,1)}), bf16[4,2,65536]{2,1,0:T(2,128)(2,1)S(1)}, u32[]{:S(2)}, u32[]{:S(2)}) async-start(bf16[4,2,65536]{2,1,0:T(2,128)(2,1)} %reshape.438), calls=%async_computation.2 | async-start | bytes 2097152 | tf_op jit(solution)/shard_map/all_to_all | solution.py:84
  62.5 4.0 collective-permute-start.11
  66.5 18.7 %collective-permute-start.12 = (bf16[128,2560]{1,0:T(8,128)(2,1)S(1)}, bf16[128,2560]{1,0:T(8,128)(2,1)S(1)}, u32[]{:S(2)}, u32[]{:S(2)}) collective-permute-start(bf16[128,2560]{1,0:T(8,128)(2,1)S(1)} %collective-permute-done.11), channel_id=1, source_target_pairs={{0,8},{8,0},{4,12},{12,4},{16,24},{24,16},{20,28},{28,20},{32,40},... | collective-permute-start | bytes 1966088 | tf_op jit(solution)/shard_map/ppermute | solution.py:19
  85.1 32.8 %collective-permute-start.13 = (bf16[128,2560]{1,0:T(8,128)(2,1)S(1)}, bf16[128,2560]{1,0:T(8,128)(2,1)S(1)}, u32[]{:S(2)}, u32[]{:S(2)}) collective-permute-start(bf16[128,2560]{1,0:T(8,128)(2,1)S(1)} %collective-permute-done.12), channel_id=1, source_target_pairs={{0,16},{16,0},{4,20},{20,4},{8,24},{24,8},{12,28},{28,12},{32,48},... | collective-permute-start | bytes 1966088 | tf_op jit(solution)/shard_map/ppermute | solution.py:19
  90.2 41.7 %collective-permute-start = (bf16[128,512]{1,0:T(8,128)(2,1)S(1)}, bf16[128,512]{1,0:T(8,128)(2,1)S(1)}, u32[]{:S(2)}, u32[]{:S(2)}) collective-permute-start(bf16[128,512]{1,0:T(8,128)(2,1)S(1)} %bitcast.384), channel_id=1, source_target_pairs={{0,44},{4,48},{8,52},{12,56},{16,60},{20,64},{24,68},{28,72},{32,7... | collective-permute-start | bytes 393224 | tf_op jit(solution)/shard_map/ppermute | solution.py:25
  117.9 66.1 %collective-permute-start.14 = (bf16[128,2560]{1,0:T(8,128)(2,1)S(1)}, bf16[128,2560]{1,0:T(8,128)(2,1)S(1)}, u32[]{:S(2)}, u32[]{:S(2)}) collective-permute-start(bf16[128,2560]{1,0:T(8,128)(2,1)S(1)} %collective-permute-done.13), channel_id=1, source_target_pairs={{0,32},{32,0},{4,36},{36,4},{8,40},{40,8},{12,44},{44,12},{16,48},... | collective-permute-start | bytes 1966088 | tf_op jit(solution)/shard_map/ppermute | solution.py:19
  126.7 37.3 %collective-permute-start.1 = (bf16[128,512]{1,0:T(8,128)(2,1)S(1)}, bf16[128,512]{1,0:T(8,128)(2,1)S(1)}, u32[]{:S(2)}, u32[]{:S(2)}) collective-permute-start(bf16[128,512]{1,0:T(8,128)(2,1)S(1)} %bitcast.385), channel_id=1, source_target_pairs={{0,40},{4,44},{8,48},{12,52},{16,56},{20,60},{24,64},{28,68},{32,7... | collective-permute-start | bytes 393224 | tf_op jit(solution)/shard_map/ppermute | solution.py:25
  128.0 50.3 %collective-permute-start.2 = (bf16[128,512]{1,0:T(8,128)(2,1)S(1)}, bf16[128,512]{1,0:T(8,128)(2,1)S(1)}, u32[]{:S(2)}, u32[]{:S(2)}) collective-permute-start(bf16[128,512]{1,0:T(8,128)(2,1)S(1)} %bitcast.386), channel_id=1, source_target_pairs={{0,36},{4,40},{8,44},{12,48},{16,52},{20,56},{24,60},{28,64},{32,6... | collective-permute-start | bytes 393224 | tf_op jit(solution)/shard_map/ppermute | solution.py:25
  129.9 56.1 %collective-permute-start.3 = (bf16[128,512]{1,0:T(8,128)(2,1)S(1)}, bf16[128,512]{1,0:T(8,128)(2,1)S(1)}, u32[]{:S(2)}, u32[]{:S(2)}) collective-permute-start(bf16[128,512]{1,0:T(8,128)(2,1)S(1)} %bitcast.387), channel_id=1, source_target_pairs={{0,32},{4,36},{8,40},{12,44},{16,48},{20,52},{24,56},{28,60},{32,6... | collective-permute-start | bytes 393224 | tf_op jit(solution)/shard_map/ppermute | solution.py:25
  131.9 65.1 %collective-permute-start.4 = (bf16[128,512]{1,0:T(8,128)(2,1)S(1)}, bf16[128,512]{1,0:T(8,128)(2,1)S(1)}, u32[]{:S(2)}, u32[]{:S(2)}) collective-permute-start(bf16[128,512]{1,0:T(8,128)(2,1)S(1)} %bitcast.388), channel_id=1, source_target_pairs={{0,28},{4,32},{8,36},{12,40},{16,44},{20,48},{24,52},{28,56},{32,6... | collective-permute-start | bytes 393224 | tf_op jit(solution)/shard_map/ppermute | solution.py:25
  164.1 56.3 %collective-permute-start.5 = (bf16[128,512]{1,0:T(8,128)(2,1)S(1)}, bf16[128,512]{1,0:T(8,128)(2,1)S(1)}, u32[]{:S(2)}, u32[]{:S(2)}) collective-permute-start(bf16[128,512]{1,0:T(8,128)(2,1)S(1)} %bitcast.389), channel_id=1, source_target_pairs={{0,24},{4,28},{8,32},{12,36},{16,40},{20,44},{24,48},{28,52},{32,5... | collective-permute-start | bytes 393224 | tf_op jit(solution)/shard_map/ppermute | solution.py:25
  178.3 53.1 %collective-permute-start.6 = (bf16[128,512]{1,0:T(8,128)(2,1)S(1)}, bf16[128,512]{1,0:T(8,128)(2,1)S(1)}, u32[]{:S(2)}, u32[]{:S(2)}) collective-permute-start(bf16[128,512]{1,0:T(8,128)(2,1)S(1)} %bitcast.390), channel_id=1, source_target_pairs={{0,20},{4,24},{8,28},{12,32},{16,36},{20,40},{24,44},{28,48},{32,5... | collective-permute-start | bytes 393224 | tf_op jit(solution)/shard_map/ppermute | solution.py:25
  184.1 42.0 %collective-permute-start.15 = (bf16[128,2560]{1,0:T(8,128)(2,1)S(1)}, bf16[128,2560]{1,0:T(8,128)(2,1)S(1)}, u32[]{:S(2)}, u32[]{:S(2)}) collective-permute-start(bf16[128,2560]{1,0:T(8,128)(2,1)S(1)} %collective-permute-done.14), channel_id=1, source_target_pairs={{0,64},{64,0},{4,68},{68,4},{8,72},{72,8},{12,76},{76,12},{16,80},... | collective-permute-start | bytes 1966088 | tf_op jit(solution)/shard_map/ppermute | solution.py:19
  186.0 47.4 %collective-permute-start.7 = (bf16[128,512]{1,0:T(8,128)(2,1)S(1)}, bf16[128,512]{1,0:T(8,128)(2,1)S(1)}, u32[]{:S(2)}, u32[]{:S(2)}) collective-permute-start(bf16[128,512]{1,0:T(8,128)(2,1)S(1)} %bitcast.391), channel_id=1, source_target_pairs={{0,16},{4,20},{8,24},{12,28},{16,32},{20,36},{24,40},{28,44},{32,4... | collective-permute-start | bytes 393224 | tf_op jit(solution)/shard_map/ppermute | solution.py:25
  197.0 68.3 %collective-permute-start.8 = (bf16[128,512]{1,0:T(8,128)(2,1)S(1)}, bf16[128,512]{1,0:T(8,128)(2,1)S(1)}, u32[]{:S(2)}, u32[]{:S(2)}) collective-permute-start(bf16[128,512]{1,0:T(8,128)(2,1)S(1)} %bitcast.392), channel_id=1, source_target_pairs={{0,12},{4,16},{8,20},{12,24},{16,28},{20,32},{24,36},{28,40},{32,4... | collective-permute-start | bytes 393224 | tf_op jit(solution)/shard_map/ppermute | solution.py:25
  220.4 45.0 %collective-permute-start.9 = (bf16[128,512]{1,0:T(8,128)(2,1)S(1)}, bf16[128,512]{1,0:T(8,128)(2,1)S(1)}, u32[]{:S(2)}, u32[]{:S(2)}) collective-permute-start(bf16[128,512]{1,0:T(8,128)(2,1)S(1)} %bitcast.393), channel_id=1, source_target_pairs={{0,8},{4,12},{8,16},{12,20},{16,24},{20,28},{24,32},{28,36},{32,40... | collective-permute-start | bytes 393224 | tf_op jit(solution)/shard_map/ppermute | solution.py:25
  226.1 33.6 %collective-permute-start.16 = (bf16[128,2560]{1,0:T(8,128)(2,1)S(1)}, bf16[128,2560]{1,0:T(8,128)(2,1)S(1)}, u32[]{:S(2)}, u32[]{:S(2)}) collective-permute-start(bf16[128,2560]{1,0:T(8,128)(2,1)S(1)} %collective-permute-done.15), channel_id=1, source_target_pairs={{0,128},{128,0},{4,132},{132,4},{8,136},{136,8},{12,140},{140,12},... | collective-permute-start | bytes 1966088 | tf_op jit(solution)/shard_map/ppermute | solution.py:19
  231.4 33.9 %collective-permute-start.10 = (bf16[128,512]{1,0:T(8,128)(2,1)S(1)}, bf16[128,512]{1,0:T(8,128)(2,1)S(1)}, u32[]{:S(2)}, u32[]{:S(2)}) collective-permute-start(bf16[128,512]{1,0:T(8,128)(2,1)S(1)} %bitcast.394), channel_id=1, source_target_pairs={{0,4},{4,8},{8,12},{12,16},{16,20},{20,24},{24,28},{28,32},{32,36}... | collective-permute-start | bytes 393224 | tf_op jit(solution)/shard_map/ppermute | solution.py:25
  259.6 35.7 %collective-permute-start.17 = (bf16[128,2560]{1,0:T(8,128)(2,1)S(1)}, bf16[128,2560]{1,0:T(8,128)(2,1)S(1)}, u32[]{:S(2)}, u32[]{:S(2)}) collective-permute-start(bf16[128,2560]{1,0:T(8,128)(2,1)S(1)} %collective-permute-done.16), channel_id=1, source_target_pairs={{0,256},{256,0},{4,260},{260,4},{8,264},{264,8},{12,268},{268,12},... | collective-permute-start | bytes 1966088 | tf_op jit(solution)/shard_map/ppermute | solution.py:19
  295.4 15.7 %collective-permute-start.18 = (bf16[2,128,512]{2,1,0:T(8,128)(2,1)S(1)}, bf16[2,128,512]{2,1,0:T(8,128)(2,1)}, u32[]{:S(2)}, u32[]{:S(2)}) collective-permute-start(bf16[2,128,512]{2,1,0:T(8,128)(2,1)S(1)} %pad_maximum_fusion.3), channel_id=1, source_target_pairs={{4,0},{8,4},{12,8},{16,12},{20,16},{24,20},{28,24},{32,28},{36,32}... | collective-permute-start | bytes 786440 | tf_op jit(solution)/shard_map/ppermute | solution.py:25
  298.4 8.3 %copy-start.3 = (bf16[23,128,512]{2,1,0:T(8,128)(2,1)}, bf16[23,128,512]{2,1,0:T(8,128)(2,1)S(1)}, u32[]{:S(2)}) copy-start(bf16[23,128,512]{2,1,0:T(8,128)(2,1)S(1)} %get-tuple-element.45) | copy-start | bytes 9043972
  298.4 10.3 %copy-start.9 = (bf16[12,128,512]{2,1,0:T(8,128)(2,1)}, bf16[12,128,512]{2,1,0:T(8,128)(2,1)S(1)}, u32[]{:S(2)}) copy-start(bf16[12,128,512]{2,1,0:T(8,128)(2,1)S(1)} %get-tuple-element.44) | copy-start | bytes 4718596
  298.4 16.5 %collective-permute-start.19 = (bf16[2,128,512]{2,1,0:T(8,128)(2,1)S(1)}, bf16[2,128,512]{2,1,0:T(8,128)(2,1)S(1)}, u32[]{:S(2)}, u32[]{:S(2)}) collective-permute-start(bf16[2,128,512]{2,1,0:T(8,128)(2,1)S(1)} %pad_maximum_fusion.3), channel_id=1, source_target_pairs={{8,0},{12,4},{16,8},{20,12},{24,16},{28,20},{32,24},{36,28},{40,32... | collective-permute-start | bytes 786440 | tf_op jit(solution)/shard_map/ppermute | solution.py:25
  302.9 15.2 %collective-permute-start.20 = (bf16[2,128,512]{2,1,0:T(8,128)(2,1)S(1)}, bf16[2,128,512]{2,1,0:T(8,128)(2,1)S(1)}, u32[]{:S(2)}, u32[]{:S(2)}) collective-permute-start(bf16[2,128,512]{2,1,0:T(8,128)(2,1)S(1)} %pad_maximum_fusion.3), channel_id=1, source_target_pairs={{12,0},{16,4},{20,8},{24,12},{28,16},{32,20},{36,24},{40,28},{44,3... | collective-permute-start | bytes 786440 | tf_op jit(solution)/shard_map/ppermute | solution.py:25
  304.8 27.9 %collective-permute-start.21 = (bf16[2,128,512]{2,1,0:T(8,128)(2,1)S(1)}, bf16[2,128,512]{2,1,0:T(8,128)(2,1)S(1)}, u32[]{:S(2)}, u32[]{:S(2)}) collective-permute-start(bf16[2,128,512]{2,1,0:T(8,128)(2,1)S(1)} %pad_maximum_fusion.3), channel_id=1, source_target_pairs={{16,0},{20,4},{24,8},{28,12},{32,16},{36,20},{40,24},{44,28},{48,3... | collective-permute-start | bytes 786440 | tf_op jit(solution)/shard_map/ppermute | solution.py:25
  306.7 98.1 %collective-permute-start.22 = (bf16[2,128,512]{2,1,0:T(8,128)(2,1)S(1)}, bf16[2,128,512]{2,1,0:T(8,128)(2,1)S(1)}, u32[]{:S(2)}, u32[]{:S(2)}) collective-permute-start(bf16[2,128,512]{2,1,0:T(8,128)(2,1)S(1)} %pad_maximum_fusion.3), channel_id=1, source_target_pairs={{20,0},{24,4},{28,8},{32,12},{36,16},{40,20},{44,24},{48,28},{52,3... | collective-permute-start | bytes 786440 | tf_op jit(solution)/shard_map/ppermute | solution.py:25
  311.1 97.7 %collective-permute-start.23 = (bf16[2,128,512]{2,1,0:T(8,128)(2,1)S(1)}, bf16[2,128,512]{2,1,0:T(8,128)(2,1)S(1)}, u32[]{:S(2)}, u32[]{:S(2)}) collective-permute-start(bf16[2,128,512]{2,1,0:T(8,128)(2,1)S(1)} %pad_maximum_fusion.3), channel_id=1, source_target_pairs={{24,0},{28,4},{32,8},{36,12},{40,16},{44,20},{48,24},{52,28},{56,3... | collective-permute-start | bytes 786440 | tf_op jit(solution)/shard_map/ppermute | solution.py:25
  314.9 99.4 %collective-permute-start.24 = (bf16[2,128,512]{2,1,0:T(8,128)(2,1)S(1)}, bf16[2,128,512]{2,1,0:T(8,128)(2,1)S(1)}, u32[]{:S(2)}, u32[]{:S(2)}) collective-permute-start(bf16[2,128,512]{2,1,0:T(8,128)(2,1)S(1)} %pad_maximum_fusion.3), channel_id=1, source_target_pairs={{28,0},{32,4},{36,8},{40,12},{44,16},{48,20},{52,24},{56,28},{60,3... | collective-permute-start | bytes 786440 | tf_op jit(solution)/shard_map/ppermute | solution.py:25
  318.0 96.9 %collective-permute-start.25 = (bf16[2,128,512]{2,1,0:T(8,128)(2,1)S(1)}, bf16[2,128,512]{2,1,0:T(8,128)(2,1)S(1)}, u32[]{:S(2)}, u32[]{:S(2)}) collective-permute-start(bf16[2,128,512]{2,1,0:T(8,128)(2,1)S(1)} %pad_maximum_fusion.3), channel_id=1, source_target_pairs={{32,0},{36,4},{40,8},{44,12},{48,16},{52,20},{56,24},{60,28},{64,3... | collective-permute-start | bytes 786440 | tf_op jit(solution)/shard_map/ppermute | solution.py:25
  332.7 82.9 %collective-permute-start.26 = (bf16[2,128,512]{2,1,0:T(8,128)(2,1)S(1)}, bf16[2,128,512]{2,1,0:T(8,128)(2,1)S(1)}, u32[]{:S(2)}, u32[]{:S(2)}) collective-permute-start(bf16[2,128,512]{2,1,0:T(8,128)(2,1)S(1)} %pad_maximum_fusion.3), channel_id=1, source_target_pairs={{36,0},{40,4},{44,8},{48,12},{52,16},{56,20},{60,24},{64,28},{68,3... | collective-permute-start | bytes 786440 | tf_op jit(solution)/shard_map/ppermute | solution.py:25
  404.8 14.7 %collective-permute-start.27 = (bf16[2,128,512]{2,1,0:T(8,128)(2,1)S(1)}, bf16[2,128,512]{2,1,0:T(8,128)(2,1)S(1)}, u32[]{:S(2)}, u32[]{:S(2)}) collective-permute-start(bf16[2,128,512]{2,1,0:T(8,128)(2,1)S(1)} %pad_maximum_fusion.3), channel_id=1, source_target_pairs={{40,0},{44,4},{48,8},{52,12},{56,16},{60,20},{64,24},{68,28},{72,3... | collective-permute-start | bytes 786440 | tf_op jit(solution)/shard_map/ppermute | solution.py:25
  408.8 26.7 %collective-permute-start.28 = (bf16[2,128,512]{2,1,0:T(8,128)(2,1)S(1)}, bf16[2,128,512]{2,1,0:T(8,128)(2,1)S(1)}, u32[]{:S(2)}, u32[]{:S(2)}) collective-permute-start(bf16[2,128,512]{2,1,0:T(8,128)(2,1)S(1)} %pad_maximum_fusion.3), channel_id=1, source_target_pairs={{44,0},{48,4},{52,8},{56,12},{60,16},{64,20},{68,24},{72,28},{76,3... | collective-permute-start | bytes 786440 | tf_op jit(solution)/shard_map/ppermute | solution.py:25
  439.5 2.6 copy-start.5
  442.1 2.6 copy-start.1
  442.1 2.6 copy-start.8
  444.6 1.6 copy-start.7
  447.7 1.6 copy-start.6
  453.7 32.0 %copy-start = (bf16[1,4,32,2048]{3,1,2,0:T(4,128)(2,1)S(1)}, bf16[1,4,32,2048]{3,1,2,0:T(4,128)(2,1)}, u32[]{:S(2)}) copy-start(bf16[1,4,32,2048]{3,1,2,0:T(4,128)(2,1)} %get-tuple-element.9) | copy-start | bytes 1572868
  455.1 58.1 %copy-start.4 = (pred[128,1536]{0,1:T(8,128)(4,1)S(1)}, pred[128,1536]{0,1:T(8,128)(4,1)}, u32[]{:S(2)}) copy-start(pred[128,1536]{0,1:T(8,128)(4,1)} %get-tuple-element.73) | copy-start | bytes 589828
  455.3 7.1 %collective-permute-start.29 = (bf16[128,2048]{1,0:T(8,128)(2,1)S(1)}, bf16[128,2048]{1,0:T(8,128)(2,1)S(1)}, u32[]{:S(2)}, u32[]{:S(2)}) collective-permute-start(bf16[128,2048]{1,0:T(8,128)(2,1)S(1)} %pad_maximum_fusion.2), channel_id=1, source_target_pairs={{0,4},{4,0},{8,12},{12,8},{16,20},{20,16},{24,28},{28,24},{32,36},... | collective-permute-start | bytes 1572872 | tf_op jit(solution)/shard_map/ppermute | solution.py:19
  462.4 21.3 %collective-permute-start.30 = (bf16[128,2048]{1,0:T(8,128)(2,1)S(1)}, bf16[128,2048]{1,0:T(8,128)(2,1)S(1)}, u32[]{:S(2)}, u32[]{:S(2)}) collective-permute-start(bf16[128,2048]{1,0:T(8,128)(2,1)S(1)} %collective-permute-done.29), channel_id=1, source_target_pairs={{0,8},{8,0},{4,12},{12,4},{16,24},{24,16},{20,28},{28,20},{32,40},... | collective-permute-start | bytes 1572872 | tf_op jit(solution)/shard_map/ppermute | solution.py:19
  483.7 27.6 %collective-permute-start.31 = (bf16[128,2048]{1,0:T(8,128)(2,1)S(1)}, bf16[128,2048]{1,0:T(8,128)(2,1)}, u32[]{:S(2)}, u32[]{:S(2)}) collective-permute-start(bf16[128,2048]{1,0:T(8,128)(2,1)S(1)} %collective-permute-done.30), channel_id=1, source_target_pairs={{0,16},{16,0},{4,20},{20,4},{8,24},{24,8},{12,28},{28,12},{32,48},... | collective-permute-start | bytes 1572872 | tf_op jit(solution)/shard_map/ppermute | solution.py:19
  511.3 27.5 %collective-permute-start.32 = (bf16[128,2048]{1,0:T(8,128)(2,1)}, bf16[128,2048]{1,0:T(8,128)(2,1)}, u32[]{:S(2)}, u32[]{:S(2)}) collective-permute-start(bf16[128,2048]{1,0:T(8,128)(2,1)} %collective-permute-done.31), channel_id=1, source_target_pairs={{0,32},{32,0},{4,36},{36,4},{8,40},{40,8},{12,44},{44,12},{16,48},... | collective-permute-start | bytes 1572872 | tf_op jit(solution)/shard_map/ppermute | solution.py:19
  513.2 2.5 copy-start.10
  538.8 31.7 %collective-permute-start.33 = (bf16[128,2048]{1,0:T(8,128)(2,1)}, bf16[128,2048]{1,0:T(8,128)(2,1)}, u32[]{:S(2)}, u32[]{:S(2)}) collective-permute-start(bf16[128,2048]{1,0:T(8,128)(2,1)} %collective-permute-done.32), channel_id=1, source_target_pairs={{0,64},{64,0},{4,68},{68,4},{8,72},{72,8},{12,76},{76,12},{16,80},... | collective-permute-start | bytes 1572872 | tf_op jit(solution)/shard_map/ppermute | solution.py:19
  570.5 31.4 %collective-permute-start.34 = (bf16[128,2048]{1,0:T(8,128)(2,1)}, bf16[128,2048]{1,0:T(8,128)(2,1)}, u32[]{:S(2)}, u32[]{:S(2)}) collective-permute-start(bf16[128,2048]{1,0:T(8,128)(2,1)} %collective-permute-done.33), channel_id=1, source_target_pairs={{0,128},{128,0},{4,132},{132,4},{8,136},{136,8},{12,140},{140,12},... | collective-permute-start | bytes 1572872 | tf_op jit(solution)/shard_map/ppermute | solution.py:19
  601.9 58.0 %collective-permute-start.35 = (bf16[128,2048]{1,0:T(8,128)(2,1)}, bf16[128,2048]{1,0:T(8,128)(2,1)S(1)}, u32[]{:S(2)}, u32[]{:S(2)}) collective-permute-start(bf16[128,2048]{1,0:T(8,128)(2,1)} %collective-permute-done.34), channel_id=1, source_target_pairs={{0,256},{256,0},{4,260},{260,4},{8,264},{264,8},{12,268},{268,12},... | collective-permute-start | bytes 1572872 | tf_op jit(solution)/shard_map/ppermute | solution.py:19
where the time goes:
time: 682 us; the launch traced here: 680 us
  starting transfers between devices  303 us (44%)
  waiting for transfers between devices  273 us (40%)
  local copies, waits for them, and re-layouts  53.2 us (8%)
  matrix products  25.2 us (4%)
  blocking collectives  17.3 us (3%)
  other arithmetic  7.01 us (1%)
    ppermute x14, waiting for transfers between devices, partner(): return lax.ppermute(block, axis, route)  210 us
    ppermute x22, starting transfers between devices, shifted(): return lax.ppermute(block, axis, route)  182 us
    ppermute x14, starting transfers between devices, partner(): return lax.ppermute(block, axis, route)  109 us
    ppermute x22, waiting for transfers between devices, shifted(): return lax.ppermute(block, axis, route)  47.8 us
    unnamed x55, local copies, waits for them, and re-layouts  30 us
    all_to_all x1, blocking collectives, per_device(): lax.all_to_all(result, 'head', split_axis=1, concat_axis=2, tiled=True)  17.3 us
  transfers between devices with their start and end apart: 39, of which 17 were waited for; matrix products, arithmetic and copies ran while one was open for 7% of the time, Pallas kernels for 0%

commit v1 on v0

--- a/solution.py
+++ b/solution.py
@@ -7,6 +7,28 @@
 HD = 128
 REACH = 11
 NEG_FILL = -1e30
+
+
+def in_blocks(array, dim, size):
+    before, after = (array.shape[:dim], array.shape[dim + 1 :])
+    return jnp.moveaxis(array.reshape(*before, size, -1, *after), dim, 0)
+
+
+def in_order(tiles, dim):
+    dims = list(tiles.shape[1:])
+    dims[dim] *= tiles.shape[0]
+    return jnp.moveaxis(tiles, 0, dim).reshape(dims)
+
+
+def rotated_exchange(value, axis, split_dim, concat_dim):
+    size, here = (lax.axis_size(axis), lax.axis_index(axis))
+    tiles = in_blocks(value, split_dim, size)
+    outs = [tiles[here]]
+    for lap in range(1, size):
+        sent = tiles[(here + lap) % size]
+        outs.append(lax.ppermute(sent, axis, [(i, (i + lap) % size) for i in range(size)]))
+    tiles = jnp.stack(outs)[(here - jnp.arange(size)) % size]
+    return in_order(tiles, concat_dim)
 
 
 def partner(block, axis, distance):
@@ -81,7 +103,7 @@
     ctx_pos = lax.axis_index("ctx")
     reach = min(REACH, ctx_count // 2)
     query_local, key_local, value_local = (
-        lax.all_to_all(queries, "head", split_axis=2, concat_axis=1, tiled=True),
+        rotated_exchange(queries, "head", 2, 1),
         lax.all_to_all(keys, "head", split_axis=2, concat_axis=1, tiled=True),
         lax.all_to_all(values, "head", split_axis=2, concat_axis=1, tiled=True),
     )

time: 682 us -> 664 us (0.974); the launches traced: 680 us -> 655 us
  waiting for transfers between devices: 273 us -> 247 us
  local copies, waits for them, and re-layouts: 53.2 us -> 37.8 us
  starting transfers between devices: 303 us -> 312 us
  matrix products: 25.2 us -> 32.5 us
    ppermute x14, waiting for transfers between devices: 210 us -> 196 us  [partner(): return lax.ppermute(block, axis, route)]
    ppermute x0 -> x3, starting transfers between devices: none -> 11.9 us  [rotated_exchange(): lax.ppermute(sent, axis, [(i, (i + lap) % size) for i in range(size)])]
    all_to_all x1 -> x0, waiting for transfers between devices: 11.6 us -> none  [per_device(): lax.all_to_all(queries, 'head', split_axis=2, concat_axis=1, tiled=True)]
    all_to_all x1 -> x0, local copies, waits for them, and re-layouts: 9.82 us -> none  [per_device(): lax.all_to_all(queries, 'head', split_axis=2, concat_axis=1, tiled=True)]
    unnamed x55 -> x56, local copies, waits for them, and re-layouts: 30 us -> 20.5 us
  transfers between devices with their start and end apart: 39 -> 41, of which waited for: 17 -> 16; matrix products, arithmetic and copies ran while one was open for 7% -> 8% of each run, Pallas kernels for 0% -> 0%
where the time goes in v1:
time: 664 us; the launch traced here: 655 us
  starting transfers between devices  312 us (47%)
  waiting for transfers between devices  247 us (37%)
  local copies, waits for them, and re-layouts  37.8 us (6%)
  matrix products  32.5 us (5%)
  blocking collectives  17.3 us (3%)
  other arithmetic  7.16 us (1%)
    ppermute x14, waiting for transfers between devices, partner(): return lax.ppermute(block, axis, route)  196 us
    ppermute x22, starting transfers between devices, shifted(): return lax.ppermute(block, axis, route)  178 us
    ppermute x14, starting transfers between devices, partner(): return lax.ppermute(block, axis, route)  114 us
    ppermute x22, waiting for transfers between devices, shifted(): return lax.ppermute(block, axis, route)  45.4 us
    unnamed x56, local copies, waits for them, and re-layouts  20.5 us
    all_to_all x1, blocking collectives, per_device(): lax.all_to_all(result, 'head', split_axis=1, concat_axis=2, tiled=True)  17.3 us
    sub x8, matrix products, attend(): weights = jnp.where(allowed[None], jnp.exp(masked - top), 0.0)  16.4 us
    dot_general x8, matrix products, attend(): jnp.einsum('hrs,sd->rhd', weights.astype(jnp.bfloat16), value_head, prefe...  16.1 us
  transfers between devices with their start and end apart: 41, of which 16 were waited for; matrix products, arithmetic and copies ran while one was open for 8% of the time, Pallas kernels for 0%

profile of v1, /device:TPU:248, one launch (start us, length us, event | category | flops | bytes accessed | tf_op | source)
XLA Modules:
  0.0 654.5 jit_solution(12660830616000918362)
XLA Ops:
  2.4 4.3 all-to-all-start
  8.5 2.3 constant_dynamic-slice_fusion.3
  11.0 3.9 collective-permute-start.11
  15.1 4.6 collective-permute-start.12
  19.9 3.4 collective-permute-start.13
  25.4 3.3 all-to-all-start.1
  29.4 5.2 all-to-all-done.1
  37.1 1.9 collective-permute-start.14
  43.3 16.4 %collective-permute-done.15 = bf16[128,2560]{1,0:T(8,128)(2,1)S(1)} collective-permute-done((bf16[128,2560]{1,0:T(8,128)(2,1)S(1)}, bf16[128,2560]{1,0:T(8,128)(2,1)S(1)}, u32[]{:S(2)}, u32[]{:S(2)}) %collective-permute-start.15) | collective-permute-done | bytes 655392 | tf_op jit(solution)/shard_map/ppermute | solution.py:41
  61.8 3.1 and_and_fusion
  66.1 26.4 %collective-permute-done.16 = bf16[128,2560]{1,0:T(8,128)(2,1)S(1)} collective-permute-done((bf16[128,2560]{1,0:T(8,128)(2,1)S(1)}, bf16[128,2560]{1,0:T(8,128)(2,1)S(1)}, u32[]{:S(2)}, u32[]{:S(2)}) %collective-permute-start.16) | collective-permute-done | bytes 655392 | tf_op jit(solution)/shard_map/ppermute | solution.py:41
  92.5 8.2 %collective-permute-start.17 = (bf16[128,2560]{1,0:T(8,128)(2,1)S(1)}, bf16[128,2560]{1,0:T(8,128)(2,1)S(1)}, u32[]{:S(2)}, u32[]{:S(2)}) collective-permute-start(bf16[128,2560]{1,0:T(8,128)(2,1)S(1)} %collective-permute-done.16), channel_id=1, source_target_pairs={{0,32},{32,0},{4,36},{36,4},{8,40},{40,8},{12,44},{44,12},{16,48},... | collective-permute-start | bytes 1966088 | tf_op jit(solution)/shard_map/ppermute | solution.py:41
  102.6 1.9 collective-permute-start.2
  104.6 1.9 collective-permute-start.3
  106.5 3.0 collective-permute-start.4
  110.2 28.5 %collective-permute-done.1 = bf16[128,512]{1,0:T(8,128)(2,1)S(1)} collective-permute-done((bf16[128,512]{1,0:T(8,128)(2,1)S(1)}, bf16[128,512]{1,0:T(8,128)(2,1)S(1)}, u32[]{:S(2)}, u32[]{:S(2)}) %collective-permute-start.1) | collective-permute-done | bytes 131104 | tf_op jit(solution)/shard_map/ppermute | solution.py:47
  138.7 13.7 %collective-permute-start.5 = (bf16[128,512]{1,0:T(8,128)(2,1)S(1)}, bf16[128,512]{1,0:T(8,128)(2,1)S(1)}, u32[]{:S(2)}, u32[]{:S(2)}) collective-permute-start(bf16[128,512]{1,0:T(8,128)(2,1)S(1)} %bitcast.401), channel_id=1, source_target_pairs={{0,24},{4,28},{8,32},{12,36},{16,40},{20,44},{24,48},{28,52},{32,5... | collective-permute-start | bytes 393224 | tf_op jit(solution)/shard_map/ppermute | solution.py:47
  153.1 5.5 collective-permute-start.6
  158.6 1.9 collective-permute-start.18
  161.2 11.0 %collective-permute-start.7 = (bf16[128,512]{1,0:T(8,128)(2,1)S(1)}, bf16[128,512]{1,0:T(8,128)(2,1)S(1)}, u32[]{:S(2)}, u32[]{:S(2)}) collective-permute-start(bf16[128,512]{1,0:T(8,128)(2,1)S(1)} %bitcast.403), channel_id=1, source_target_pairs={{0,16},{4,20},{8,24},{12,28},{16,32},{20,36},{24,40},{28,44},{32,4... | collective-permute-start | bytes 393224 | tf_op jit(solution)/shard_map/ppermute | solution.py:47
  172.8 23.4 %collective-permute-start.8 = (bf16[128,512]{1,0:T(8,128)(2,1)S(1)}, bf16[128,512]{1,0:T(8,128)(2,1)S(1)}, u32[]{:S(2)}, u32[]{:S(2)}) collective-permute-start(bf16[128,512]{1,0:T(8,128)(2,1)S(1)} %bitcast.404), channel_id=1, source_target_pairs={{0,12},{4,16},{8,20},{12,24},{16,28},{20,32},{24,36},{28,40},{32,4... | collective-permute-start | bytes 393224 | tf_op jit(solution)/shard_map/ppermute | solution.py:47
  196.9 5.6 collective-permute-start.9
  202.5 5.2 collective-permute-start.19
  208.4 1.9 collective-permute-start.10
  211.7 24.3 %collective-permute-done.19 = bf16[128,2560]{1,0:T(8,128)(2,1)S(1)} collective-permute-done((bf16[128,2560]{1,0:T(8,128)(2,1)S(1)}, bf16[128,2560]{1,0:T(8,128)(2,1)S(1)}, u32[]{:S(2)}, u32[]{:S(2)}) %collective-permute-start.19) | collective-permute-done | bytes 655392 | tf_op jit(solution)/shard_map/ppermute | solution.py:41
  236.0 5.9 collective-permute-start.20
  244.0 28.0 %collective-permute-done.20 = bf16[128,2560]{1,0:T(8,128)(2,1)S(1)} collective-permute-done((bf16[128,2560]{1,0:T(8,128)(2,1)S(1)}, bf16[128,2560]{1,0:T(8,128)(2,1)S(1)}, u32[]{:S(2)}, u32[]{:S(2)}) %collective-permute-start.20) | collective-permute-done | bytes 655392 | tf_op jit(solution)/shard_map/ppermute | solution.py:41
  272.0 3.8 collective-permute-start.21
  276.5 3.6 collective-permute-start.22
  280.1 1.9 collective-permute-start.23
  282.0 1.9 collective-permute-start.24
  284.0 1.9 collective-permute-start.25
  288.3 2.1 collective-permute-start.26
  292.1 2.9 collective-permute-start.27
  295.6 6.6 %collective-permute-done.23 = bf16[2,128,512]{2,1,0:T(8,128)(2,1)S(1)} collective-permute-done((bf16[2,128,512]{2,1,0:T(8,128)(2,1)S(1)}, bf16[2,128,512]{2,1,0:T(8,128)(2,1)S(1)}, u32[]{:S(2)}, u32[]{:S(2)}) %collective-permute-start.23) | collective-permute-done | bytes 262176 | tf_op jit(solution)/shard_map/ppermute | solution.py:47
  302.3 6.7 %collective-permute-start.28 = (bf16[2,128,512]{2,1,0:T(8,128)(2,1)S(1)}, bf16[2,128,512]{2,1,0:T(8,128)(2,1)S(1)}, u32[]{:S(2)}, u32[]{:S(2)}) collective-permute-start(bf16[2,128,512]{2,1,0:T(8,128)(2,1)S(1)} %pad_maximum_fusion.4), channel_id=1, source_target_pairs={{32,0},{36,4},{40,8},{44,12},{48,16},{52,20},{56,24},{60,28},{64,3... | collective-permute-start | bytes 786440 | tf_op jit(solution)/shard_map/ppermute | solution.py:47
  309.7 43.2 %collective-permute-start.29 = (bf16[2,128,512]{2,1,0:T(8,128)(2,1)S(1)}, bf16[2,128,512]{2,1,0:T(8,128)(2,1)S(1)}, u32[]{:S(2)}, u32[]{:S(2)}) collective-permute-start(bf16[2,128,512]{2,1,0:T(8,128)(2,1)S(1)} %pad_maximum_fusion.4), channel_id=1, source_target_pairs={{36,0},{40,4},{44,8},{48,12},{52,16},{56,20},{60,24},{64,28},{68,3... | collective-permute-start | bytes 786440 | tf_op jit(solution)/shard_map/ppermute | solution.py:47
  353.6 4.2 collective-permute-start.30
  358.5 35.1 %collective-permute-start.31 = (bf16[2,128,512]{2,1,0:T(8,128)(2,1)S(1)}, bf16[2,128,512]{2,1,0:T(8,128)(2,1)S(1)}, u32[]{:S(2)}, u32[]{:S(2)}) collective-permute-start(bf16[2,128,512]{2,1,0:T(8,128)(2,1)S(1)} %pad_maximum_fusion.4), channel_id=1, source_target_pairs={{44,0},{48,4},{52,8},{56,12},{60,16},{64,20},{68,24},{72,28},{76,3... | collective-permute-start | bytes 786440 | tf_op jit(solution)/shard_map/ppermute | solution.py:47
  396.9 10.2 %collective-permute-done.31 = bf16[2,128,512]{2,1,0:T(8,128)(2,1)S(1)} collective-permute-done((bf16[2,128,512]{2,1,0:T(8,128)(2,1)S(1)}, bf16[2,128,512]{2,1,0:T(8,128)(2,1)S(1)}, u32[]{:S(2)}, u32[]{:S(2)}) %collective-permute-start.31) | collective-permute-done | bytes 262176 | tf_op jit(solution)/shard_map/ppermute | solution.py:47
  408.6 2.5 gather_fusion.2
  411.1 2.6 fusion.48
  413.7 2.6 fusion.224
  427.0 2.1 collective-permute-start.32
  430.9 7.4 %collective-permute-start.33 = (bf16[128,2048]{1,0:T(8,128)(2,1)S(1)}, bf16[128,2048]{1,0:T(8,128)(2,1)S(1)}, u32[]{:S(2)}, u32[]{:S(2)}) collective-permute-start(bf16[128,2048]{1,0:T(8,128)(2,1)S(1)} %collective-permute-done.32), channel_id=1, source_target_pairs={{0,8},{8,0},{4,12},{12,4},{16,24},{24,16},{20,28},{28,20},{32,40},... | collective-permute-start | bytes 1572872 | tf_op jit(solution)/shard_map/ppermute | solution.py:41
  438.4 12.2 %collective-permute-done.33 = bf16[128,2048]{1,0:T(8,128)(2,1)S(1)} collective-permute-done((bf16[128,2048]{1,0:T(8,128)(2,1)S(1)}, bf16[128,2048]{1,0:T(8,128)(2,1)S(1)}, u32[]{:S(2)}, u32[]{:S(2)}) %collective-permute-start.33) | collective-permute-done | bytes 524320 | tf_op jit(solution)/shard_map/ppermute | solution.py:41
  450.6 5.5 collective-permute-start.34
  456.3 22.7 %collective-permute-done.34 = bf16[128,2048]{1,0:T(8,128)(2,1)S(1)} collective-permute-done((bf16[128,2048]{1,0:T(8,128)(2,1)S(1)}, bf16[128,2048]{1,0:T(8,128)(2,1)S(1)}, u32[]{:S(2)}, u32[]{:S(2)}) %collective-permute-start.34) | collective-permute-done | bytes 524320 | tf_op jit(solution)/shard_map/ppermute | solution.py:41
  480.9 2.4 fusion.228
  483.3 2.6 fusion.134
  486.1 21.0 %collective-permute-done.35 = bf16[128,2048]{1,0:T(8,128)(2,1)S(1)} collective-permute-done((bf16[128,2048]{1,0:T(8,128)(2,1)S(1)}, bf16[128,2048]{1,0:T(8,128)(2,1)S(1)}, u32[]{:S(2)}, u32[]{:S(2)}) %collective-permute-start.35) | collective-permute-done | bytes 524320 | tf_op jit(solution)/shard_map/ppermute | solution.py:41
  507.1 21.3 %collective-permute-start.36 = (bf16[128,2048]{1,0:T(8,128)(2,1)S(1)}, bf16[128,2048]{1,0:T(8,128)(2,1)S(1)}, u32[]{:S(2)}, u32[]{:S(2)}) collective-permute-start(bf16[128,2048]{1,0:T(8,128)(2,1)S(1)} %collective-permute-done.35), channel_id=1, source_target_pairs={{0,64},{64,0},{4,68},{68,4},{8,72},{72,8},{12,76},{76,12},{16,80},... | collective-permute-start | bytes 1572872 | tf_op jit(solution)/shard_map/ppermute | solution.py:41
  528.5 2.4 fusion.227
  530.9 2.6 fusion.131
  533.7 6.9 %collective-permute-done.36 = bf16[128,2048]{1,0:T(8,128)(2,1)S(1)} collective-permute-done((bf16[128,2048]{1,0:T(8,128)(2,1)S(1)}, bf16[128,2048]{1,0:T(8,128)(2,1)S(1)}, u32[]{:S(2)}, u32[]{:S(2)}) %collective-permute-start.36) | collective-permute-done | bytes 524320 | tf_op jit(solution)/shard_map/ppermute | solution.py:41
  540.6 16.9 %collective-permute-start.37 = (bf16[128,2048]{1,0:T(8,128)(2,1)S(1)}, bf16[128,2048]{1,0:T(8,128)(2,1)S(1)}, u32[]{:S(2)}, u32[]{:S(2)}) collective-permute-start(bf16[128,2048]{1,0:T(8,128)(2,1)S(1)} %collective-permute-done.36), channel_id=1, source_target_pairs={{0,128},{128,0},{4,132},{132,4},{8,136},{136,8},{12,140},{140,12},... | collective-permute-start | bytes 1572872 | tf_op jit(solution)/shard_map/ppermute | solution.py:41
  557.5 2.4 fusion.226
  559.9 2.6 fusion.128
  562.7 16.6 %collective-permute-done.37 = bf16[128,2048]{1,0:T(8,128)(2,1)S(1)} collective-permute-done((bf16[128,2048]{1,0:T(8,128)(2,1)S(1)}, bf16[128,2048]{1,0:T(8,128)(2,1)S(1)}, u32[]{:S(2)}, u32[]{:S(2)}) %collective-permute-start.37) | collective-permute-done | bytes 524320 | tf_op jit(solution)/shard_map/ppermute | solution.py:41
  579.3 32.0 %collective-permute-start.38 = (bf16[128,2048]{1,0:T(8,128)(2,1)S(1)}, bf16[128,2048]{1,0:T(8,128)(2,1)S(1)}, u32[]{:S(2)}, u32[]{:S(2)}) collective-permute-start(bf16[128,2048]{1,0:T(8,128)(2,1)S(1)} %collective-permute-done.37), channel_id=1, source_target_pairs={{0,256},{256,0},{4,260},{260,4},{8,264},{264,8},{12,268},{268,12},... | collective-permute-start | bytes 1572872 | tf_op jit(solution)/shard_map/ppermute | solution.py:41
  611.3 2.4 fusion.225
  613.7 2.6 fusion.125
  616.4 18.1 %collective-permute-done.38 = bf16[128,2048]{1,0:T(8,128)(2,1)S(1)} collective-permute-done((bf16[128,2048]{1,0:T(8,128)(2,1)S(1)}, bf16[128,2048]{1,0:T(8,128)(2,1)S(1)}, u32[]{:S(2)}, u32[]{:S(2)}) %collective-permute-start.38) | collective-permute-done | bytes 524320 | tf_op jit(solution)/shard_map/ppermute | solution.py:41
  635.6 17.3 %all_to_all.54 = bf16[2,128,2048]{2,0,1:T(2,128)(2,1)S(1)} all-to-all(bf16[2,128,2048]{2,0,1:T(2,128)(2,1)S(1)} %copy.300), channel_id=1, replica_groups=mesh['ctx'=128,'head'=4] {'head'}, dimensions={1} | all-to-all | bytes 2097152 | tf_op jit(solution)/shard_map/all_to_all | solution.py:152
  (149 shorter events, 56.6 us)
Async XLA Ops:
  2.4 23.0 %all-to-all-start = ((bf16[4,2,8192]{2,1,0:T(2,128)(2,1)}), bf16[4,2,8192]{2,1,0:T(2,128)(2,1)S(1)}, u32[]{:S(2)}, u32[]{:S(2)}) async-start(bf16[4,2,8192]{2,1,0:T(2,128)(2,1)} %reshape.503), calls=%async_computation | async-start | bytes 262144 | tf_op jit(solution)/shard_map/all_to_all | solution.py:107
  8.5 14.8 %copy-start.5 = (bf16[2,32,1024]{2,1,0:T(8,128)(2,1)S(1)}, bf16[2,32,1024]{2,1,0:T(8,128)(2,1)}, u32[]{:S(2)}) copy-start(bf16[2,32,1024]{2,1,0:T(8,128)(2,1)} %param.6) | copy-start | bytes 393220
  10.8 14.2 %copy-start.9 = (s32[47]{0:T(128)S(1)}, s32[47]{0:T(128)}, u32[]{:S(2)}) copy-start(s32[47]{0:T(128)} %param.7) | copy-start | bytes 568
  11.0 24.4 %collective-permute-start.11 = (bf16[2,32,2048]{2,1,0:T(8,128)(2,1)S(1)}, bf16[2,32,2048]{2,1,0:T(8,128)(2,1)S(1)}, u32[]{:S(2)}, u32[]{:S(2)}) collective-permute-start(bf16[2,32,2048]{2,1,0:T(8,128)(2,1)S(1)} %bitcast.413), channel_id=1, source_target_pairs={{0,1},{1,2},{2,3},{3,0},{4,5},{5,6},{6,7},{7,4},{8,9},{9,10},{10,1... | collective-permute-start | bytes 786440 | tf_op jit(solution)/shard_map/ppermute | solution.py:29
  15.1 20.3 %collective-permute-start.12 = (bf16[2,32,2048]{2,1,0:T(8,128)(2,1)S(1)}, bf16[2,32,2048]{2,1,0:T(8,128)(2,1)S(1)}, u32[]{:S(2)}, u32[]{:S(2)}) collective-permute-start(bf16[2,32,2048]{2,1,0:T(8,128)(2,1)S(1)} %bitcast.414), channel_id=1, source_target_pairs={{0,2},{1,3},{2,0},{3,1},{4,6},{5,7},{6,4},{7,5},{8,10},{9,11},{10,... | collective-permute-start | bytes 786440 | tf_op jit(solution)/shard_map/ppermute | solution.py:29
  19.9 15.5 %collective-permute-start.13 = (bf16[2,32,2048]{2,1,0:T(8,128)(2,1)S(1)}, bf16[2,32,2048]{2,1,0:T(8,128)(2,1)S(1)}, u32[]{:S(2)}, u32[]{:S(2)}) collective-permute-start(bf16[2,32,2048]{2,1,0:T(8,128)(2,1)S(1)} %bitcast.415), channel_id=1, source_target_pairs={{0,3},{1,0},{2,1},{3,2},{4,7},{5,4},{6,5},{7,6},{8,11},{9,8},{10,9... | collective-permute-start | bytes 786440 | tf_op jit(solution)/shard_map/ppermute | solution.py:29
  25.4 9.3 %all-to-all-start.1 = ((bf16[4,2,8192]{2,1,0:T(2,128)(2,1)}), bf16[4,2,8192]{2,1,0:T(2,128)(2,1)S(1)}, u32[]{:S(2)}, u32[]{:S(2)}) async-start(bf16[4,2,8192]{2,1,0:T(2,128)(2,1)} %reshape.505), calls=%async_computation.1 | async-start | bytes 262144 | tf_op jit(solution)/shard_map/all_to_all | solution.py:108
  37.1 4.0 collective-permute-start.14
  41.1 18.7 %collective-permute-start.15 = (bf16[128,2560]{1,0:T(8,128)(2,1)S(1)}, bf16[128,2560]{1,0:T(8,128)(2,1)S(1)}, u32[]{:S(2)}, u32[]{:S(2)}) collective-permute-start(bf16[128,2560]{1,0:T(8,128)(2,1)S(1)} %collective-permute-done.14), channel_id=1, source_target_pairs={{0,8},{8,0},{4,12},{12,4},{16,24},{24,16},{20,28},{28,20},{32,40},... | collective-permute-start | bytes 1966088 | tf_op jit(solution)/shard_map/ppermute | solution.py:41
  59.8 32.8 %collective-permute-start.16 = (bf16[128,2560]{1,0:T(8,128)(2,1)S(1)}, bf16[128,2560]{1,0:T(8,128)(2,1)S(1)}, u32[]{:S(2)}, u32[]{:S(2)}) collective-permute-start(bf16[128,2560]{1,0:T(8,128)(2,1)S(1)} %collective-permute-done.15), channel_id=1, source_target_pairs={{0,16},{16,0},{4,20},{20,4},{8,24},{24,8},{12,28},{28,12},{32,48},... | collective-permute-start | bytes 1966088 | tf_op jit(solution)/shard_map/ppermute | solution.py:41
  64.8 41.7 %collective-permute-start = (bf16[128,512]{1,0:T(8,128)(2,1)S(1)}, bf16[128,512]{1,0:T(8,128)(2,1)S(1)}, u32[]{:S(2)}, u32[]{:S(2)}) collective-permute-start(bf16[128,512]{1,0:T(8,128)(2,1)S(1)} %bitcast.396), channel_id=1, source_target_pairs={{0,44},{4,48},{8,52},{12,56},{16,60},{20,64},{24,68},{28,72},{32,7... | collective-permute-start | bytes 393224 | tf_op jit(solution)/shard_map/ppermute | solution.py:47
  92.5 66.0 %collective-permute-start.17 = (bf16[128,2560]{1,0:T(8,128)(2,1)S(1)}, bf16[128,2560]{1,0:T(8,128)(2,1)S(1)}, u32[]{:S(2)}, u32[]{:S(2)}) collective-permute-start(bf16[128,2560]{1,0:T(8,128)(2,1)S(1)} %collective-permute-done.16), channel_id=1, source_target_pairs={{0,32},{32,0},{4,36},{36,4},{8,40},{40,8},{12,44},{44,12},{16,48},... | collective-permute-start | bytes 1966088 | tf_op jit(solution)/shard_map/ppermute | solution.py:41
  101.3 37.3 %collective-permute-start.1 = (bf16[128,512]{1,0:T(8,128)(2,1)S(1)}, bf16[128,512]{1,0:T(8,128)(2,1)S(1)}, u32[]{:S(2)}, u32[]{:S(2)}) collective-permute-start(bf16[128,512]{1,0:T(8,128)(2,1)S(1)} %bitcast.397), channel_id=1, source_target_pairs={{0,40},{4,44},{8,48},{12,52},{16,56},{20,60},{24,64},{28,68},{32,7... | collective-permute-start | bytes 393224 | tf_op jit(solution)/shard_map/ppermute | solution.py:47
  102.6 50.4 %collective-permute-start.2 = (bf16[128,512]{1,0:T(8,128)(2,1)S(1)}, bf16[128,512]{1,0:T(8,128)(2,1)S(1)}, u32[]{:S(2)}, u32[]{:S(2)}) collective-permute-start(bf16[128,512]{1,0:T(8,128)(2,1)S(1)} %bitcast.398), channel_id=1, source_target_pairs={{0,36},{4,40},{8,44},{12,48},{16,52},{20,56},{24,60},{28,64},{32,6... | collective-permute-start | bytes 393224 | tf_op jit(solution)/shard_map/ppermute | solution.py:47
  104.6 56.6 %collective-permute-start.3 = (bf16[128,512]{1,0:T(8,128)(2,1)S(1)}, bf16[128,512]{1,0:T(8,128)(2,1)S(1)}, u32[]{:S(2)}, u32[]{:S(2)}) collective-permute-start(bf16[128,512]{1,0:T(8,128)(2,1)S(1)} %bitcast.399), channel_id=1, source_target_pairs={{0,32},{4,36},{8,40},{12,44},{16,48},{20,52},{24,56},{28,60},{32,6... | collective-permute-start | bytes 393224 | tf_op jit(solution)/shard_map/ppermute | solution.py:47
  106.5 66.3 %collective-permute-start.4 = (bf16[128,512]{1,0:T(8,128)(2,1)S(1)}, bf16[128,512]{1,0:T(8,128)(2,1)S(1)}, u32[]{:S(2)}, u32[]{:S(2)}) collective-permute-start(bf16[128,512]{1,0:T(8,128)(2,1)S(1)} %bitcast.400), channel_id=1, source_target_pairs={{0,28},{4,32},{8,36},{12,40},{16,44},{20,48},{24,52},{28,56},{32,6... | collective-permute-start | bytes 393224 | tf_op jit(solution)/shard_map/ppermute | solution.py:47
  138.7 58.2 %collective-permute-start.5 = (bf16[128,512]{1,0:T(8,128)(2,1)S(1)}, bf16[128,512]{1,0:T(8,128)(2,1)S(1)}, u32[]{:S(2)}, u32[]{:S(2)}) collective-permute-start(bf16[128,512]{1,0:T(8,128)(2,1)S(1)} %bitcast.401), channel_id=1, source_target_pairs={{0,24},{4,28},{8,32},{12,36},{16,40},{20,44},{24,48},{28,52},{32,5... | collective-permute-start | bytes 393224 | tf_op jit(solution)/shard_map/ppermute | solution.py:47
  153.1 55.4 %collective-permute-start.6 = (bf16[128,512]{1,0:T(8,128)(2,1)S(1)}, bf16[128,512]{1,0:T(8,128)(2,1)S(1)}, u32[]{:S(2)}, u32[]{:S(2)}) collective-permute-start(bf16[128,512]{1,0:T(8,128)(2,1)S(1)} %bitcast.402), channel_id=1, source_target_pairs={{0,20},{4,24},{8,28},{12,32},{16,36},{20,40},{24,44},{28,48},{32,5... | collective-permute-start | bytes 393224 | tf_op jit(solution)/shard_map/ppermute | solution.py:47
  158.6 44.0 %collective-permute-start.18 = (bf16[128,2560]{1,0:T(8,128)(2,1)S(1)}, bf16[128,2560]{1,0:T(8,128)(2,1)S(1)}, u32[]{:S(2)}, u32[]{:S(2)}) collective-permute-start(bf16[128,2560]{1,0:T(8,128)(2,1)S(1)} %collective-permute-done.17), channel_id=1, source_target_pairs={{0,64},{64,0},{4,68},{68,4},{8,72},{72,8},{12,76},{76,12},{16,80},... | collective-permute-start | bytes 1966088 | tf_op jit(solution)/shard_map/ppermute | solution.py:41
  161.2 49.9 %collective-permute-start.7 = (bf16[128,512]{1,0:T(8,128)(2,1)S(1)}, bf16[128,512]{1,0:T(8,128)(2,1)S(1)}, u32[]{:S(2)}, u32[]{:S(2)}) collective-permute-start(bf16[128,512]{1,0:T(8,128)(2,1)S(1)} %bitcast.403), channel_id=1, source_target_pairs={{0,16},{4,20},{8,24},{12,28},{16,32},{20,36},{24,40},{28,44},{32,4... | collective-permute-start | bytes 393224 | tf_op jit(solution)/shard_map/ppermute | solution.py:47
  172.8 69.1 %collective-permute-start.8 = (bf16[128,512]{1,0:T(8,128)(2,1)S(1)}, bf16[128,512]{1,0:T(8,128)(2,1)S(1)}, u32[]{:S(2)}, u32[]{:S(2)}) collective-permute-start(bf16[128,512]{1,0:T(8,128)(2,1)S(1)} %bitcast.404), channel_id=1, source_target_pairs={{0,12},{4,16},{8,20},{12,24},{16,28},{20,32},{24,36},{28,40},{32,4... | collective-permute-start | bytes 393224 | tf_op jit(solution)/shard_map/ppermute | solution.py:47
  196.9 45.8 %collective-permute-start.9 = (bf16[128,512]{1,0:T(8,128)(2,1)S(1)}, bf16[128,512]{1,0:T(8,128)(2,1)S(1)}, u32[]{:S(2)}, u32[]{:S(2)}) collective-permute-start(bf16[128,512]{1,0:T(8,128)(2,1)S(1)} %bitcast.405), channel_id=1, source_target_pairs={{0,8},{4,12},{8,16},{12,20},{16,24},{20,28},{24,32},{28,36},{32,40... | collective-permute-start | bytes 393224 | tf_op jit(solution)/shard_map/ppermute | solution.py:47
  202.5 33.5 %collective-permute-start.19 = (bf16[128,2560]{1,0:T(8,128)(2,1)S(1)}, bf16[128,2560]{1,0:T(8,128)(2,1)S(1)}, u32[]{:S(2)}, u32[]{:S(2)}) collective-permute-start(bf16[128,2560]{1,0:T(8,128)(2,1)S(1)} %collective-permute-done.18), channel_id=1, source_target_pairs={{0,128},{128,0},{4,132},{132,4},{8,136},{136,8},{12,140},{140,12},... | collective-permute-start | bytes 1966088 | tf_op jit(solution)/shard_map/ppermute | solution.py:41
  208.4 34.9 %collective-permute-start.10 = (bf16[128,512]{1,0:T(8,128)(2,1)S(1)}, bf16[128,512]{1,0:T(8,128)(2,1)S(1)}, u32[]{:S(2)}, u32[]{:S(2)}) collective-permute-start(bf16[128,512]{1,0:T(8,128)(2,1)S(1)} %bitcast.406), channel_id=1, source_target_pairs={{0,4},{4,8},{8,12},{12,16},{16,20},{20,24},{24,28},{28,32},{32,36}... | collective-permute-start | bytes 393224 | tf_op jit(solution)/shard_map/ppermute | solution.py:47
  236.0 35.9 %collective-permute-start.20 = (bf16[128,2560]{1,0:T(8,128)(2,1)S(1)}, bf16[128,2560]{1,0:T(8,128)(2,1)S(1)}, u32[]{:S(2)}, u32[]{:S(2)}) collective-permute-start(bf16[128,2560]{1,0:T(8,128)(2,1)S(1)} %collective-permute-done.19), channel_id=1, source_target_pairs={{0,256},{256,0},{4,260},{260,4},{8,264},{264,8},{12,268},{268,12},... | collective-permute-start | bytes 1966088 | tf_op jit(solution)/shard_map/ppermute | solution.py:41
  272.0 16.3 %collective-permute-start.21 = (bf16[2,128,512]{2,1,0:T(8,128)(2,1)S(1)}, bf16[2,128,512]{2,1,0:T(8,128)(2,1)}, u32[]{:S(2)}, u32[]{:S(2)}) collective-permute-start(bf16[2,128,512]{2,1,0:T(8,128)(2,1)S(1)} %pad_maximum_fusion.4), channel_id=1, source_target_pairs={{4,0},{8,4},{12,8},{16,12},{20,16},{24,20},{28,24},{32,28},{36,32}... | collective-permute-start | bytes 786440 | tf_op jit(solution)/shard_map/ppermute | solution.py:47
  276.5 7.5 %copy-start.2 = (bf16[23,128,512]{2,1,0:T(8,128)(2,1)}, bf16[23,128,512]{2,1,0:T(8,128)(2,1)S(1)}, u32[]{:S(2)}) copy-start(bf16[23,128,512]{2,1,0:T(8,128)(2,1)S(1)} %get-tuple-element.49) | copy-start | bytes 9043972
  276.5 15.6 %collective-permute-start.22 = (bf16[2,128,512]{2,1,0:T(8,128)(2,1)S(1)}, bf16[2,128,512]{2,1,0:T(8,128)(2,1)S(1)}, u32[]{:S(2)}, u32[]{:S(2)}) collective-permute-start(bf16[2,128,512]{2,1,0:T(8,128)(2,1)S(1)} %pad_maximum_fusion.4), channel_id=1, source_target_pairs={{8,0},{12,4},{16,8},{20,12},{24,16},{28,20},{32,24},{36,28},{40,32... | collective-permute-start | bytes 786440 | tf_op jit(solution)/shard_map/ppermute | solution.py:47
  280.1 22.2 %collective-permute-start.23 = (bf16[2,128,512]{2,1,0:T(8,128)(2,1)S(1)}, bf16[2,128,512]{2,1,0:T(8,128)(2,1)S(1)}, u32[]{:S(2)}, u32[]{:S(2)}) collective-permute-start(bf16[2,128,512]{2,1,0:T(8,128)(2,1)S(1)} %pad_maximum_fusion.4), channel_id=1, source_target_pairs={{12,0},{16,4},{20,8},{24,12},{28,16},{32,20},{36,24},{40,28},{44,3... | collective-permute-start | bytes 786440 | tf_op jit(solution)/shard_map/ppermute | solution.py:47
  282.0 27.7 %collective-permute-start.24 = (bf16[2,128,512]{2,1,0:T(8,128)(2,1)S(1)}, bf16[2,128,512]{2,1,0:T(8,128)(2,1)S(1)}, u32[]{:S(2)}, u32[]{:S(2)}) collective-permute-start(bf16[2,128,512]{2,1,0:T(8,128)(2,1)S(1)} %pad_maximum_fusion.4), channel_id=1, source_target_pairs={{16,0},{20,4},{24,8},{28,12},{32,16},{36,20},{40,24},{44,28},{48,3... | collective-permute-start | bytes 786440 | tf_op jit(solution)/shard_map/ppermute | solution.py:47
  284.0 69.6 %collective-permute-start.25 = (bf16[2,128,512]{2,1,0:T(8,128)(2,1)S(1)}, bf16[2,128,512]{2,1,0:T(8,128)(2,1)S(1)}, u32[]{:S(2)}, u32[]{:S(2)}) collective-permute-start(bf16[2,128,512]{2,1,0:T(8,128)(2,1)S(1)} %pad_maximum_fusion.4), channel_id=1, source_target_pairs={{20,0},{24,4},{28,8},{32,12},{36,16},{40,20},{44,24},{48,28},{52,3... | collective-permute-start | bytes 786440 | tf_op jit(solution)/shard_map/ppermute | solution.py:47
  288.3 70.2 %collective-permute-start.26 = (bf16[2,128,512]{2,1,0:T(8,128)(2,1)S(1)}, bf16[2,128,512]{2,1,0:T(8,128)(2,1)S(1)}, u32[]{:S(2)}, u32[]{:S(2)}) collective-permute-start(bf16[2,128,512]{2,1,0:T(8,128)(2,1)S(1)} %pad_maximum_fusion.4), channel_id=1, source_target_pairs={{24,0},{28,4},{32,8},{36,12},{40,16},{44,20},{48,24},{52,28},{56,3... | collective-permute-start | bytes 786440 | tf_op jit(solution)/shard_map/ppermute | solution.py:47
  292.1 102.2 %collective-permute-start.27 = (bf16[2,128,512]{2,1,0:T(8,128)(2,1)S(1)}, bf16[2,128,512]{2,1,0:T(8,128)(2,1)S(1)}, u32[]{:S(2)}, u32[]{:S(2)}) collective-permute-start(bf16[2,128,512]{2,1,0:T(8,128)(2,1)S(1)} %pad_maximum_fusion.4), channel_id=1, source_target_pairs={{28,0},{32,4},{36,8},{40,12},{44,16},{48,20},{52,24},{56,28},{60,3... | collective-permute-start | bytes 786440 | tf_op jit(solution)/shard_map/ppermute | solution.py:47
  302.3 92.6 %collective-permute-start.28 = (bf16[2,128,512]{2,1,0:T(8,128)(2,1)S(1)}, bf16[2,128,512]{2,1,0:T(8,128)(2,1)S(1)}, u32[]{:S(2)}, u32[]{:S(2)}) collective-permute-start(bf16[2,128,512]{2,1,0:T(8,128)(2,1)S(1)} %pad_maximum_fusion.4), channel_id=1, source_target_pairs={{32,0},{36,4},{40,8},{44,12},{48,16},{52,20},{56,24},{60,28},{64,3... | collective-permute-start | bytes 786440 | tf_op jit(solution)/shard_map/ppermute | solution.py:47
  309.7 85.9 %collective-permute-start.29 = (bf16[2,128,512]{2,1,0:T(8,128)(2,1)S(1)}, bf16[2,128,512]{2,1,0:T(8,128)(2,1)S(1)}, u32[]{:S(2)}, u32[]{:S(2)}) collective-permute-start(bf16[2,128,512]{2,1,0:T(8,128)(2,1)S(1)} %pad_maximum_fusion.4), channel_id=1, source_target_pairs={{36,0},{40,4},{44,8},{48,12},{52,16},{56,20},{60,24},{64,28},{68,3... | collective-permute-start | bytes 786440 | tf_op jit(solution)/shard_map/ppermute | solution.py:47
  353.6 42.7 %collective-permute-start.30 = (bf16[2,128,512]{2,1,0:T(8,128)(2,1)S(1)}, bf16[2,128,512]{2,1,0:T(8,128)(2,1)S(1)}, u32[]{:S(2)}, u32[]{:S(2)}) collective-permute-start(bf16[2,128,512]{2,1,0:T(8,128)(2,1)S(1)} %pad_maximum_fusion.4), channel_id=1, source_target_pairs={{40,0},{44,4},{48,8},{52,12},{56,16},{60,20},{64,24},{68,28},{72,3... | collective-permute-start | bytes 786440 | tf_op jit(solution)/shard_map/ppermute | solution.py:47
  358.5 48.7 %collective-permute-start.31 = (bf16[2,128,512]{2,1,0:T(8,128)(2,1)S(1)}, bf16[2,128,512]{2,1,0:T(8,128)(2,1)S(1)}, u32[]{:S(2)}, u32[]{:S(2)}) collective-permute-start(bf16[2,128,512]{2,1,0:T(8,128)(2,1)S(1)} %pad_maximum_fusion.4), channel_id=1, source_target_pairs={{44,0},{48,4},{52,8},{56,12},{60,16},{64,20},{68,24},{72,28},{76,3... | collective-permute-start | bytes 786440 | tf_op jit(solution)/shard_map/ppermute | solution.py:47
  411.1 2.6 copy-start.4
  413.7 2.6 copy-start.1
  413.7 2.6 copy-start.8
  416.3 1.6 copy-start.7
  419.3 1.6 copy-start.6
  425.3 30.8 %copy-start = (bf16[1,4,32,2048]{3,2,0,1:T(8,128)(2,1)S(1)}, bf16[1,4,32,2048]{3,2,0,1:T(8,128)(2,1)}, u32[]{:S(2)}) copy-start(bf16[1,4,32,2048]{3,2,0,1:T(8,128)(2,1)} %get-tuple-element.9) | copy-start | bytes 1572868
  425.3 55.5 %copy-start.3 = (pred[128,1536]{0,1:T(8,128)(4,1)S(1)}, pred[128,1536]{0,1:T(8,128)(4,1)}, u32[]{:S(2)}) copy-start(pred[128,1536]{0,1:T(8,128)(4,1)} %get-tuple-element.77) | copy-start | bytes 589828
  427.0 4.0 collective-permute-start.32
  430.9 19.7 %collective-permute-start.33 = (bf16[128,2048]{1,0:T(8,128)(2,1)S(1)}, bf16[128,2048]{1,0:T(8,128)(2,1)S(1)}, u32[]{:S(2)}, u32[]{:S(2)}) collective-permute-start(bf16[128,2048]{1,0:T(8,128)(2,1)S(1)} %collective-permute-done.32), channel_id=1, source_target_pairs={{0,8},{8,0},{4,12},{12,4},{16,24},{24,16},{20,28},{28,20},{32,40},... | collective-permute-start | bytes 1572872 | tf_op jit(solution)/shard_map/ppermute | solution.py:41
  450.6 28.3 %collective-permute-start.34 = (bf16[128,2048]{1,0:T(8,128)(2,1)S(1)}, bf16[128,2048]{1,0:T(8,128)(2,1)S(1)}, u32[]{:S(2)}, u32[]{:S(2)}) collective-permute-start(bf16[128,2048]{1,0:T(8,128)(2,1)S(1)} %collective-permute-done.33), channel_id=1, source_target_pairs={{0,16},{16,0},{4,20},{20,4},{8,24},{24,8},{12,28},{28,12},{32,48},... | collective-permute-start | bytes 1572872 | tf_op jit(solution)/shard_map/ppermute | solution.py:41
  478.9 28.2 %collective-permute-start.35 = (bf16[128,2048]{1,0:T(8,128)(2,1)S(1)}, bf16[128,2048]{1,0:T(8,128)(2,1)S(1)}, u32[]{:S(2)}, u32[]{:S(2)}) collective-permute-start(bf16[128,2048]{1,0:T(8,128)(2,1)S(1)} %collective-permute-done.34), channel_id=1, source_target_pairs={{0,32},{32,0},{4,36},{36,4},{8,40},{40,8},{12,44},{44,12},{16,48},... | collective-permute-start | bytes 1572872 | tf_op jit(solution)/shard_map/ppermute | solution.py:41
  507.1 33.4 %collective-permute-start.36 = (bf16[128,2048]{1,0:T(8,128)(2,1)S(1)}, bf16[128,2048]{1,0:T(8,128)(2,1)S(1)}, u32[]{:S(2)}, u32[]{:S(2)}) collective-permute-start(bf16[128,2048]{1,0:T(8,128)(2,1)S(1)} %collective-permute-done.35), channel_id=1, source_target_pairs={{0,64},{64,0},{4,68},{68,4},{8,72},{72,8},{12,76},{76,12},{16,80},... | collective-permute-start | bytes 1572872 | tf_op jit(solution)/shard_map/ppermute | solution.py:41
  540.6 38.7 %collective-permute-start.37 = (bf16[128,2048]{1,0:T(8,128)(2,1)S(1)}, bf16[128,2048]{1,0:T(8,128)(2,1)S(1)}, u32[]{:S(2)}, u32[]{:S(2)}) collective-permute-start(bf16[128,2048]{1,0:T(8,128)(2,1)S(1)} %collective-permute-done.36), channel_id=1, source_target_pairs={{0,128},{128,0},{4,132},{132,4},{8,136},{136,8},{12,140},{140,12},... | collective-permute-start | bytes 1572872 | tf_op jit(solution)/shard_map/ppermute | solution.py:41
  579.3 55.2 %collective-permute-start.38 = (bf16[128,2048]{1,0:T(8,128)(2,1)S(1)}, bf16[128,2048]{1,0:T(8,128)(2,1)S(1)}, u32[]{:S(2)}, u32[]{:S(2)}) collective-permute-start(bf16[128,2048]{1,0:T(8,128)(2,1)S(1)} %collective-permute-done.37), channel_id=1, source_target_pairs={{0,256},{256,0},{4,260},{260,4},{8,264},{264,8},{12,268},{268,12},... | collective-permute-start | bytes 1572872 | tf_op jit(solution)/shard_map/ppermute | solution.py:41
